TPU v7x, 32 devices: a whole 2x2x4 slice. The times are simulated.
32 devices in a mesh: group: 2 (over x), space: 16 (over z, y, core).
Axes of the slice: x: 2, y: 2, z: 4, core: 2. Of those that a mesh axis runs over, the one named last changes fastest.
Arguments:
- snapshots: bfloat16 [32, 3, 256, 128], P('group', None, 'space'), parts along dimension 0, may hold values from -8 to 8
- basis: bfloat16 [128, 3, 128, 256], P('group', None, 'space'), parts along dimension 0, may hold values from -6 to 6
- mode_weights: float32 [128], P('group'), parts along dimension 0, may hold values from 0.5 to 4
- land_mask: int32 [256, 128], P('space'), may hold values 0 or 1
- scale_index: int32 [128], replicated, may hold values from 0 to 15
- scale_values: float32 [16], replicated, may hold values from 0.06 to 0.24
Outputs:
- new_basis: bfloat16 [128, 3, 128, 256], P('group', None, 'space'), parts along dimension 0
- coefficients: float32 [32, 64], P('group'), parts along dimension 0
There are 2 independent parts, one for each index of `group`. A program takes and returns all parts, laid end to end along the dimension named above; an argument that names none is the same for every part. Nothing has to cross between parts.
Inputs may be any that keep to these rules, and one draw needn't show every extreme that they name: `land_mask`: 1 marks ocean, 0 land. Row y uses scale_values[scale_index[y]].
All inputs are finite; a program needn't handle non-finite values. No bound on the sum of `land_mask` on one device may be relied on, other than what follows from the above.
Results may differ from a plain program's by a relative error of at most 0.0057.
Values may be sent and summed in bfloat16 or wider, within the bound.
A program may use at most 128 MiB of HBM per device.

v0:
```python
import math

import jax
import jax.numpy as jnp
from jax import lax
from jax.sharding import PartitionSpec as P

PASS_COEFS = (1.0, 0.95, 0.85, 0.7, 0.5, 0.3)


def with_halo(cells, sides, width):
    for axis, dim in sides:
        count = lax.axis_size(axis)
        head = lax.slice_in_dim(cells, 0, width, axis=dim)
        tail = lax.slice_in_dim(cells, cells.shape[dim] - width, cells.shape[dim], axis=dim)
        cells = jnp.concatenate(
            [
                lax.ppermute(tail, axis, [(i, (i + 1) % count) for i in range(count)]),
                cells,
                lax.ppermute(head, axis, [((i + 1) % count, i) for i in range(count)]),
            ],
            axis=dim,
        )
    return cells


def latitude_scale(scale_index, scale_values):
    levels = jnp.arange(scale_values.shape[0], dtype=jnp.int32)
    matches = (scale_index[None, :] == levels[:, None]).astype(jnp.float32)
    return jnp.sum(matches * scale_values[:, None], axis=0)


def masked_step(fields_now, ocean, factor):
    centre = fields_now[:, :, 1:-1]
    m_centre = ocean[1:-1]
    east_flux = ocean[2:] * (fields_now[:, :, 2:] - centre)
    west_flux = ocean[:-2] * (fields_now[:, :, :-2] - centre)
    padded = jnp.pad(centre, ((0, 0), (0, 0), (0, 0), (1, 1)))
    m_pad = jnp.pad(m_centre, ((0, 0), (1, 1)))
    north_flux = m_pad[:, 2:] * (padded[..., 2:] - centre)
    south_flux = m_pad[:, :-2] * (padded[..., :-2] - centre)
    return centre + factor * (m_centre * (east_flux + west_flux + north_flux + south_flux))


def dot_rows(left, right):
    return lax.dot_general(
        left, right, (((1,), (1,)), ((), ())), preferred_element_type=jnp.float32
    )


def eof_update(data_rows, basis_rows, mode_weights, total_cells):
    high = lax.Precision.HIGHEST
    root_total = math.sqrt(total_cells)
    cross_sum = lax.psum(dot_rows(data_rows, basis_rows), "space")
    coefficients = cross_sum / root_total
    coeff_b = coefficients.astype(jnp.bfloat16)
    update = mode_weights[:, None] * basis_rows.astype(jnp.float32) + lax.dot_general(
        coeff_b, data_rows, (((0,), (0,)), ((), ())), preferred_element_type=jnp.float32
    )
    gram_matrix = lax.psum(jnp.dot(update, update.T, precision=high), "space") / total_cells
    chol_factor = jnp.linalg.cholesky(gram_matrix)
    solved = jax.scipy.linalg.solve_triangular(chol_factor, update, lower=True)
    return (solved.astype(jnp.bfloat16), coefficients)


def local(snapshots, basis, mode_weights, land_mask, scale_index, scale_values):
    lat_scale = latitude_scale(scale_index, scale_values)
    halo_width = 1
    ocean_wide = with_halo(land_mask, (("space", 0),), halo_width).astype(jnp.float32)
    fields_now = snapshots.astype(jnp.float32)
    for group_start in range(0, len(PASS_COEFS), halo_width):
        extended = with_halo(fields_now, (("space", 2),), 1)
        factor = PASS_COEFS[group_start] * lat_scale
        extended = masked_step(extended, ocean_wide, factor)
        fields_now = extended
    ocean = land_mask.astype(jnp.float32)
    filtered = (ocean * fields_now).astype(jnp.bfloat16)
    modes = basis.shape[0]
    snaps = filtered.shape[0]
    slab_data = lax.all_to_all(filtered, "space", split_axis=3, concat_axis=2, tiled=True)
    data_rows = jnp.swapaxes(slab_data, 2, 3).reshape(snaps, -1)
    basis_rows = basis.reshape(modes, -1)
    total_cells = float(data_rows.shape[1] * lax.axis_size("space"))
    solved, coefficients = eof_update(data_rows, basis_rows, mode_weights, total_cells)
    new_basis = solved.reshape(basis.shape)
    return (new_basis, coefficients)


def solution(mesh):
    placed = (
        P("group", None, "space", None),
        P("group", None, "space", None),
        P("group"),
        P("space", None),
        P(),
        P(),
    )
    return jax.shard_map(
        local,
        mesh=mesh,
        in_specs=placed,
        out_specs=(P("group", None, "space", None), P("group", None)),
        check_vma=False,
    )
```

profile of v0, /device:TPU:0, one launch (start us, length us, event | category | flops | bytes accessed | tf_op | source)
XLA Modules:
  0.0 175.6 jit_solution(13503581497344326809)
XLA Ops:
  0.6 0.7 fusion.94
  1.3 0.5 collective-permute-start
  1.8 5.0 %collective-permute-start.1 = (s32[1,128]{1,0:T(1,128)S(1)}, s32[1,128]{1,0:T(1,128)S(1)}, u32[]{:S(2)}, u32[]{:S(2)}) collective-permute-start(s32[1,128]{1,0:T(1,128)S(1)} %get-tuple-element.20), channel_id=1, source_target_pairs={{1,0},{2,1},{3,2},{4,3},{5,4},{6,5},{7,6},{8,7},{9,8},{10,9},{11,1... | collective-permute-start | bytes 1544 | tf_op jit(solution)/shard_map/ppermute | solution.py:20
  6.8 1.0 copy_convert_fusion
  7.8 0.7 collective-permute-start.2
  8.5 0.7 add_convert_fusion
  9.2 0.8 pad_slice_fusion.13
  10.0 4.4 %collective-permute-done.3 = f32[16,3,1,128]{3,0,2,1:T(8,128)S(1)} collective-permute-done((f32[16,3,1,128]{3,0,2,1:T(8,128)S(1)}, f32[16,3,1,128]{3,0,2,1:T(8,128)S(1)}, u32[]{:S(2)}, u32[]{:S(2)}) %collective-permute-start.3) | collective-permute-done | bytes 24608 | tf_op jit(solution)/shard_map/ppermute | solution.py:18
  14.4 1.2 convert_add_fusion
  15.8 0.5 collective-permute-start.5
  16.3 1.0 collective-permute-done.4
  17.3 4.6 %collective-permute-done.5 = f32[16,3,1,128]{3,0,2,1:T(8,128)S(1)} collective-permute-done((f32[16,3,1,128]{3,0,2,1:T(8,128)S(1)}, f32[16,3,1,128]{3,0,2,1:T(8,128)S(1)}, u32[]{:S(2)}, u32[]{:S(2)}) %collective-permute-start.5) | collective-permute-done | bytes 24608 | tf_op jit(solution)/shard_map/ppermute | solution.py:18
  21.8 0.3 fusion.16
  22.2 0.5 collective-permute-start.7
  22.7 1.0 collective-permute-done.6
  23.7 4.5 %collective-permute-done.7 = f32[16,3,1,128]{3,0,2,1:T(8,128)S(1)} collective-permute-done((f32[16,3,1,128]{3,0,2,1:T(8,128)S(1)}, f32[16,3,1,128]{3,0,2,1:T(8,128)S(1)}, u32[]{:S(2)}, u32[]{:S(2)}) %collective-permute-start.7) | collective-permute-done | bytes 24608 | tf_op jit(solution)/shard_map/ppermute | solution.py:18
  28.3 0.3 fusion.25
  28.6 0.5 collective-permute-start.9
  29.1 1.0 collective-permute-done.8
  30.1 4.5 %collective-permute-done.9 = f32[16,3,1,128]{3,0,2,1:T(8,128)S(1)} collective-permute-done((f32[16,3,1,128]{3,0,2,1:T(8,128)S(1)}, f32[16,3,1,128]{3,0,2,1:T(8,128)S(1)}, u32[]{:S(2)}, u32[]{:S(2)}) %collective-permute-start.9) | collective-permute-done | bytes 24608 | tf_op jit(solution)/shard_map/ppermute | solution.py:18
  34.7 0.3 fusion.34
  35.1 0.5 collective-permute-start.11
  35.5 1.0 collective-permute-done.10
  36.6 4.5 %collective-permute-done.11 = f32[16,3,1,128]{3,0,2,1:T(8,128)S(1)} collective-permute-done((f32[16,3,1,128]{3,0,2,1:T(8,128)S(1)}, f32[16,3,1,128]{3,0,2,1:T(8,128)S(1)}, u32[]{:S(2)}, u32[]{:S(2)}) %collective-permute-start.11) | collective-permute-done | bytes 24608 | tf_op jit(solution)/shard_map/ppermute | solution.py:18
  41.1 0.3 fusion.43
  41.5 0.5 collective-permute-start.13
  42.0 1.0 collective-permute-done.12
  43.0 4.5 %collective-permute-done.13 = f32[16,3,1,128]{3,0,2,1:T(8,128)S(1)} collective-permute-done((f32[16,3,1,128]{3,0,2,1:T(8,128)S(1)}, f32[16,3,1,128]{3,0,2,1:T(8,128)S(1)}, u32[]{:S(2)}, u32[]{:S(2)}) %collective-permute-start.13) | collective-permute-done | bytes 24608 | tf_op jit(solution)/shard_map/ppermute | solution.py:18
  47.5 0.3 fusion.54
  47.8 1.1 copy.41
  48.9 2.3 %reshape.52 = bf16[16,2,3072]{2,1,0:T(2,128)(2,1)} reshape(bf16[128,3,16,16]{3,2,1,0:T(8,128)(2,1)S(1)} %bitcast.42) | data formatting | bytes 393216
  51.2 3.5 %all-to-all-start = ((bf16[16,2,3072]{2,1,0:T(2,128)(2,1)}), bf16[16,2,3072]{2,1,0:T(2,128)(2,1)S(1)}, u32[]{:S(2)}, u32[]{:S(2)}) async-start(bf16[16,2,3072]{2,1,0:T(2,128)(2,1)} %reshape.52), calls=%async_computation | async-start | bytes 393216 | tf_op jit(solution)/shard_map/all_to_all | solution.py:80
  54.9 8.8 %all-to-all-done = bf16[16,2,3072]{2,1,0:T(2,128)(2,1)S(1)} async-done(((bf16[16,2,3072]{2,1,0:T(2,128)(2,1)}), bf16[16,2,3072]{2,1,0:T(2,128)(2,1)S(1)}, u32[]{:S(2)}, u32[]{:S(2)}) %all-to-all-start) | async-done | bytes 196640 | tf_op jit(solution)/shard_map/all_to_all | solution.py:80
  63.7 1.2 reshape.53
  64.9 2.2 %copy.43 = bf16[16,3,16,16,8]{3,2,0,4,1:T(8,128)(2,1)} copy(bf16[16,3,16,16,8]{3,0,1,4,2:T(8,128)(2,1)S(1)} %bitcast.43) | data formatting | bytes 393216 | tf_op jit(solution)/shard_map/all_to_all | solution.py:80
  67.1 2.7 %all_to_all.16 = bf16[16,3,256,8]{2,0,3,1:T(8,128)(2,1)S(1)} reshape(bf16[16,3,16,16,8]{3,2,0,4,1:T(8,128)(2,1)} %copy.43) | data formatting | bytes 393216 | tf_op jit(solution)/shard_map/all_to_all | solution.py:80
  69.8 0.3 convolution_bitcast_fusion
  70.1 31.0 %psum.14 = f32[16,64]{1,0:T(8,128)S(1)} all-reduce(f32[16,64]{1,0:T(8,128)S(1)} %convolution_bitcast_fusion), channel_id=1, replica_groups=mesh['group'=2,'space'=16] {'space'}, use_global_device_ids=true, to_apply=%region_1.2 | all-reduce | flops 1024 | bytes 8192 | tf_op jit(solution)/shard_map/psum | solution.py:54
  101.1 0.4 convolution_add_fusion
  101.5 0.2 copy-done.3
  101.7 1.4 fusion.95
  103.1 57.8 %psum.15 = f32[64,64]{0,1:T(8,128)S(1)} all-reduce(f32[64,64]{0,1:T(8,128)S(1)} %fusion.95), channel_id=1, replica_groups=mesh['group'=2,'space'=16] {'space'}, use_global_device_ids=true, to_apply=%region_2.3 | all-reduce | flops 4096 | bytes 32768 | tf_op jit(solution)/shard_map/psum | solution.py:60
  161.0 5.8 %cholesky.16 = f32[64,64]{1,0:T(8,128)S(1)} custom-call(f32[64,64]{1,0:T(8,128)S(1)} %fusion.84), custom_call_target="Cholesky" | custom-call | tf_op jit(solution)/shard_map/jit(cholesky)/cholesky | solution.py:61
  166.9 0.6 compare_reduce_fusion
  167.5 0.7 fusion.82
  168.2 4.9 %custom-call.7 = f32[1,64,64]{1,2,0:T(8,128)S(1)} custom-call(f32[1,64,64]{2,1,0:T(8,128)S(1)} %fusion.82), custom_call_target="InvertDiagBlocksLowerTriangular" | custom-call | tf_op jit(solution)/shard_map/jit(_solve_triangular)/triangular_solve | solution.py:62
  173.1 1.5 convolution_convert_fusion
  174.6 1.0 copy.53
  (34 shorter events, 0.7 us)
Async XLA Ops:
  1.3 7.2 %collective-permute-start = (s32[1,128]{1,0:T(1,128)S(1)}, s32[1,128]{1,0:T(1,128)S(1)}, u32[]{:S(2)}, u32[]{:S(2)}) collective-permute-start(s32[1,128]{1,0:T(1,128)S(1)} %get-tuple-element.19), channel_id=1, source_target_pairs={{0,1},{1,2},{2,3},{3,4},{4,5},{5,6},{6,7},{7,8},{8,9},{9,10},{10,1... | collective-permute-start | bytes 1544 | tf_op jit(solution)/shard_map/ppermute | solution.py:18
  1.8 6.7 %collective-permute-start.1 = (s32[1,128]{1,0:T(1,128)S(1)}, s32[1,128]{1,0:T(1,128)S(1)}, u32[]{:S(2)}, u32[]{:S(2)}) collective-permute-start(s32[1,128]{1,0:T(1,128)S(1)} %get-tuple-element.20), channel_id=1, source_target_pairs={{1,0},{2,1},{3,2},{4,3},{5,4},{6,5},{7,6},{8,7},{9,8},{10,9},{11,1... | collective-permute-start | bytes 1544 | tf_op jit(solution)/shard_map/ppermute | solution.py:20
  7.8 2.2 %collective-permute-start.2 = (f32[16,3,1,128]{3,0,2,1:T(8,128)S(1)}, f32[16,3,1,128]{3,0,2,1:T(8,128)S(1)}, u32[]{:S(2)}, u32[]{:S(2)}) collective-permute-start(f32[16,3,1,128]{3,0,2,1:T(8,128)S(1)} %get-tuple-element.12), channel_id=1, source_target_pairs={{1,0},{2,1},{3,2},{4,3},{5,4},{6,5},{7,6},{8,7},{9,8},{10,9},{11,1... | collective-permute-start | bytes 73736 | tf_op jit(solution)/shard_map/ppermute | solution.py:20
  8.5 5.9 %collective-permute-start.3 = (f32[16,3,1,128]{3,0,2,1:T(8,128)S(1)}, f32[16,3,1,128]{3,0,2,1:T(8,128)S(1)}, u32[]{:S(2)}, u32[]{:S(2)}) collective-permute-start(f32[16,3,1,128]{3,0,2,1:T(8,128)S(1)} %get-tuple-element.13), channel_id=1, source_target_pairs={{0,1},{1,2},{2,3},{3,4},{4,5},{5,6},{6,7},{7,8},{8,9},{9,10},{10,1... | collective-permute-start | bytes 73736 | tf_op jit(solution)/shard_map/ppermute | solution.py:18
  15.7 1.6 collective-permute-start.4
  15.8 6.1 %collective-permute-start.5 = (f32[16,3,1,128]{3,0,2,1:T(8,128)S(1)}, f32[16,3,1,128]{3,0,2,1:T(8,128)S(1)}, u32[]{:S(2)}, u32[]{:S(2)}) collective-permute-start(f32[16,3,1,128]{3,0,2,1:T(8,128)S(1)} %get-tuple-element.11), channel_id=1, source_target_pairs={{0,1},{1,2},{2,3},{3,4},{4,5},{5,6},{6,7},{7,8},{8,9},{9,10},{10,1... | collective-permute-start | bytes 73736 | tf_op jit(solution)/shard_map/ppermute | solution.py:18
  22.1 19.9 %copy-start.2 = (s32[16,128]{1,0:T(8,128)S(1)}, s32[16,128]{1,0:T(8,128)}, u32[]{:S(2)}) copy-start(s32[16,128]{1,0:T(8,128)} %param.9) | copy-start | bytes 24580
  22.1 1.6 collective-permute-start.6
  22.2 6.1 %collective-permute-start.7 = (f32[16,3,1,128]{3,0,2,1:T(8,128)S(1)}, f32[16,3,1,128]{3,0,2,1:T(8,128)S(1)}, u32[]{:S(2)}, u32[]{:S(2)}) collective-permute-start(f32[16,3,1,128]{3,0,2,1:T(8,128)S(1)} %get-tuple-element.9), channel_id=1, source_target_pairs={{0,1},{1,2},{2,3},{3,4},{4,5},{5,6},{6,7},{7,8},{8,9},{9,10},{10,1... | collective-permute-start | bytes 73736 | tf_op jit(solution)/shard_map/ppermute | solution.py:18
  28.6 1.6 collective-permute-start.8
  28.6 6.1 %collective-permute-start.9 = (f32[16,3,1,128]{3,0,2,1:T(8,128)S(1)}, f32[16,3,1,128]{3,0,2,1:T(8,128)S(1)}, u32[]{:S(2)}, u32[]{:S(2)}) collective-permute-start(f32[16,3,1,128]{3,0,2,1:T(8,128)S(1)} %get-tuple-element.7), channel_id=1, source_target_pairs={{0,1},{1,2},{2,3},{3,4},{4,5},{5,6},{6,7},{7,8},{8,9},{9,10},{10,1... | collective-permute-start | bytes 73736 | tf_op jit(solution)/shard_map/ppermute | solution.py:18
  35.0 1.6 collective-permute-start.10
  35.1 6.1 %collective-permute-start.11 = (f32[16,3,1,128]{3,0,2,1:T(8,128)S(1)}, f32[16,3,1,128]{3,0,2,1:T(8,128)S(1)}, u32[]{:S(2)}, u32[]{:S(2)}) collective-permute-start(f32[16,3,1,128]{3,0,2,1:T(8,128)S(1)} %get-tuple-element.5), channel_id=1, source_target_pairs={{0,1},{1,2},{2,3},{3,4},{4,5},{5,6},{6,7},{7,8},{8,9},{9,10},{10,1... | collective-permute-start | bytes 73736 | tf_op jit(solution)/shard_map/ppermute | solution.py:18
  41.4 1.6 collective-permute-start.12
  41.5 6.0 %collective-permute-start.13 = (f32[16,3,1,128]{3,0,2,1:T(8,128)S(1)}, f32[16,3,1,128]{3,0,2,1:T(8,128)S(1)}, u32[]{:S(2)}, u32[]{:S(2)}) collective-permute-start(f32[16,3,1,128]{3,0,2,1:T(8,128)S(1)} %get-tuple-element.3), channel_id=1, source_target_pairs={{0,1},{1,2},{2,3},{3,4},{4,5},{5,6},{6,7},{7,8},{8,9},{9,10},{10,1... | collective-permute-start | bytes 73736 | tf_op jit(solution)/shard_map/ppermute | solution.py:18
  47.8 7.0 %copy-start = (bf16[64,3,8,256]{3,2,1,0:T(8,128)(2,1)S(1)}, bf16[64,3,8,256]{3,2,1,0:T(8,128)(2,1)}, u32[]{:S(2)}) copy-start(bf16[64,3,8,256]{3,2,1,0:T(8,128)(2,1)} %param.7) | copy-start | bytes 2359300
  51.2 12.5 %all-to-all-start = ((bf16[16,2,3072]{2,1,0:T(2,128)(2,1)}), bf16[16,2,3072]{2,1,0:T(2,128)(2,1)S(1)}, u32[]{:S(2)}, u32[]{:S(2)}) async-start(bf16[16,2,3072]{2,1,0:T(2,128)(2,1)} %reshape.52), calls=%async_computation | async-start | bytes 393216 | tf_op jit(solution)/shard_map/all_to_all | solution.py:80
  67.1 2.7 %copy-start.1 = (bf16[64,3,8,256]{3,2,1,0:T(8,128)(2,1)S(1)}, bf16[64,3,8,256]{3,2,1,0:T(8,128)(2,1)}, u32[]{:S(2)}) copy-start(bf16[64,3,8,256]{3,2,1,0:T(8,128)(2,1)} %param.7) | copy-start | bytes 2359300
  67.1 34.0 %copy-start.4 = (f32[64]{0:T(128)S(1)}, f32[64]{0:T(128)}, u32[]{:S(2)}) copy-start(f32[64]{0:T(128)} %param.8) | copy-start | bytes 772
  101.1 0.6 copy-start.3
where the time goes:
time: 176 us
  blocking collectives  88.8 us (50%)
  waiting for transfers between devices  41 us (23%)
  other arithmetic  17.2 us (10%)
  starting transfers between devices  12.5 us (7%)
  local copies, waits for them, and re-layouts  11.7 us (7%)
  matrix products  3.56 us (2%)
    psum x1, blocking collectives, eof_update(): lax.psum(jnp.dot(update, update.T, precision=high), 'space') / total_cells  57.8 us
    psum x1, blocking collectives, eof_update(): cross_sum = lax.psum(dot_rows(data_rows, basis_rows), 'space')  31 us
    ppermute x7, waiting for transfers between devices, with_halo(): lax.ppermute(tail, axis, [(i, (i + 1) % count) for i in range(count)])  27.1 us
    all_to_all x1, waiting for transfers between devices, local(): lax.all_to_all(filtered, 'space', split_axis=3, concat_axis=2, tiled=True)  8.79 us
    another operation x3, other arithmetic, eof_update(): chol_factor = jnp.linalg.cholesky(gram_matrix)  6.52 us
    ppermute x7, starting transfers between devices, with_halo(): lax.ppermute(head, axis, [((i + 1) % count, i) for i in range(count)])  6.01 us
    another operation x2, other arithmetic, eof_update(): solved = jax.scipy.linalg.solve_triangular(chol_factor, update, lower=True)  5.55 us
    ppermute x7, waiting for transfers between devices, with_halo(): lax.ppermute(head, axis, [((i + 1) % count, i) for i in range(count)])  5.11 us
  transfers between devices with their start and end apart: 15, of which 12 were waited for; matrix products, arithmetic and copies ran while one was open for 1% of the time, Pallas kernels for 0%

commit v1 on v0

v1 whole, which is shorter than its diff:
```python
import functools
import math

import jax
import jax.numpy as jnp
from jax import lax
from jax.experimental import pallas as pl
from jax.experimental.pallas import tpu as pltpu
from jax.sharding import PartitionSpec as P

PASS_COEFS = (1.0, 0.95, 0.85, 0.7, 0.5, 0.3)
HALO = len(PASS_COEFS)
LANES = 128
HIGH = lax.Precision.HIGHEST
MESH = pl.DeviceIdType.MESH
VMEM = pl.BlockSpec(memory_space=pltpu.VMEM)


def peer(step, n):
    return lax.rem(lax.axis_index("space") + step, n)


def greet(n):
    group = lax.axis_index("group")
    barrier = pltpu.get_barrier_semaphore()

    def signal(step, carry):
        pl.semaphore_signal(barrier, inc=1, device_id=(group, peer(step, n)), device_id_type=MESH)
        return carry

    lax.fori_loop(1, n, signal, 0)
    pl.semaphore_wait(barrier, n - 1)


def exchange(n, make_copy):
    def start(step, carry):
        make_copy(peer(step, n), lax.axis_index("space")).start()
        return carry

    def wait_recv(step, carry):
        source = peer(n - step, n)
        make_copy(source, source).wait_recv()
        return carry

    def wait_send(step, carry):
        make_copy(peer(step, n), lax.axis_index("space")).wait_send()
        return carry

    lax.fori_loop(1, n, start, 0)
    return lambda: lax.fori_loop(1, n, wait_recv, 0), lambda: lax.fori_loop(1, n, wait_send, 0)


def spread_kernel(n, cols, send_ref, recv_ref, land, send_sem, recv_sem):
    me = lax.axis_index("space")
    group = lax.axis_index("group")
    greet(n)

    def make_copy(dst, slot):
        return pltpu.make_async_remote_copy(
            src_ref=send_ref.at[:, :, pl.ds(pl.multiple_of(dst * LANES, LANES), LANES)],
            dst_ref=land.at[:, pl.ds(pl.multiple_of(slot * cols, cols), cols), :],
            send_sem=send_sem.at[dst],
            recv_sem=recv_sem.at[slot],
            device_id=(group, dst),
            device_id_type=MESH,
        )

    arrived, sent = exchange(n, make_copy)
    land[:, pl.ds(pl.multiple_of(me * cols, cols), cols), :] = send_ref[
        :, :, pl.ds(pl.multiple_of(me * LANES, LANES), LANES)
    ]
    arrived()
    recv_ref[...] = land[...]
    sent()


def sum_kernel(n, part_ref, total_ref, land, send_sem, recv_sem):
    me = lax.axis_index("space")
    group = lax.axis_index("group")
    greet(n)

    def make_copy(dst, slot):
        return pltpu.make_async_remote_copy(
            src_ref=part_ref,
            dst_ref=land.at[slot],
            send_sem=send_sem.at[dst],
            recv_sem=recv_sem.at[slot],
            device_id=(group, dst),
            device_id_type=MESH,
        )

    arrived, sent = exchange(n, make_copy)
    land[me] = part_ref[...]
    arrived()
    total = land[0]
    for slot in range(1, n):
        total = total + land[slot]
    total_ref[...] = total
    sent()


def filter_kernel(win, groups, recv_ref, basis_ref, index_ref, values_ref, rows_ref, gram_ref, stack, weight):
    tiles = recv_ref.shape[0] - 1
    nx = recv_ref.shape[1]
    own = win - 2 * HALO
    ny = index_ref.shape[1]
    modes_rows = basis_ref.shape[0]
    total_rows, fy_count = rows_ref.shape[0], rows_ref.shape[1] // nx
    me = lax.axis_index("space")

    for c in range(nx // LANES):
        stack[c, 0:modes_rows, :] = basis_ref[:, c * LANES : (c + 1) * LANES].astype(jnp.float32)

    lat = jnp.zeros((1, ny), jnp.float32)
    for level in range(values_ref.shape[1]):
        lat = lat + jnp.where(index_ref[...] == level, values_ref[0:1, level : level + 1], 0.0)
    lane = lax.broadcasted_iota(jnp.int32, (ny, LANES), 1)
    row = lax.broadcasted_iota(jnp.int32, (ny, LANES), 0)
    pick = jnp.zeros((ny, LANES), jnp.float32)
    for g in range(groups):
        here = (lane >= g * win) & (lane < (g + 1) * win)
        pick = jnp.where(here & (row == me * own - HALO + lane - g * win), 1.0, pick)
    lat_lane = jnp.dot(jnp.broadcast_to(lat, (8, ny)), pick, precision=HIGH, preferred_element_type=jnp.float32)[0:1]

    def east(a):
        return pltpu.roll(a, nx - 1, 0)

    def west(a):
        return pltpu.roll(a, 1, 0)

    def north(a):
        return pltpu.roll(a, LANES - 1, 1)

    def south(a):
        return pltpu.roll(a, 1, 1)

    ocean = recv_ref[tiles].astype(jnp.float32)
    base = ocean * lat_lane
    sides = (east, west, north, south)
    for i, side in enumerate(sides):
        weight[i] = base * side(ocean)
    weight[4] = ocean

    @pl.loop(0, tiles)
    def _(t):
        f = recv_ref[t].astype(jnp.float32)
        for coef in PASS_COEFS:
            flux = weight[0] * (east(f) - f)
            for i in range(1, 4):
                flux = flux + weight[i] * (sides[i](f) - f)
            f = f + coef * flux
        f = (weight[4] * f).astype(jnp.bfloat16).astype(jnp.float32)
        turned = f.T
        for g in range(groups):
            at = pl.multiple_of(modes_rows + (t * groups + g) * own, own)
            block = turned[g * win + HALO : g * win + HALO + own, :]
            for c in range(nx // LANES):
                stack[c, pl.ds(at, own), :] = block[:, c * LANES : (c + 1) * LANES]

    for fy in range(fy_count):
        for c in range(nx // LANES):
            at = fy * nx + c * LANES
            rows_ref[:, at : at + LANES] = stack[c, pl.ds(fy, total_rows, stride=fy_count), :].astype(jnp.bfloat16)
    gram_ref[...] = jnp.zeros_like(gram_ref)
    gram_ref[:, 0:total_rows] = lax.dot_general(
        rows_ref[...], rows_ref[...], (((1,), (1,)), ((), ())), preferred_element_type=jnp.float32
    )


def solve_kernel(total_cells, nx, gram_ref, weights_ref, rows_ref, basis_ref, coef_ref, k_t, full, out):
    modes = weights_ref.shape[1]
    total_rows = gram_ref.shape[0]
    fy_count = rows_ref.shape[1] // nx
    eye = (
        lax.broadcasted_iota(jnp.int32, (modes, modes), 0) == lax.broadcasted_iota(jnp.int32, (modes, modes), 1)
    )
    full[...] = jnp.zeros_like(full)
    full[0:total_rows, :] = gram_ref[...]
    coefficients = full[modes:total_rows, 0:modes] * (1.0 / math.sqrt(total_cells))
    coef_ref[...] = coefficients
    k_t[...] = jnp.zeros_like(k_t)
    k_t[0:modes, 0:modes] = jnp.where(eye, weights_ref[...], 0.0)
    k_t[modes:total_rows, 0:modes] = coefficients.astype(jnp.bfloat16).astype(jnp.float32)
    k = k_t[...].T
    half = jnp.dot(full[...], k_t[...], precision=HIGH, preferred_element_type=jnp.float32)
    gram = jnp.dot(k, half, precision=HIGH, preferred_element_type=jnp.float32)[0:modes, 0:modes] * (1.0 / total_cells)

    a = jnp.concatenate([gram, jnp.where(eye, 1.0, 0.0)], axis=1)
    done = []
    for j in range(modes):
        top = j % 8
        row = a[top : top + 1, :]
        factor = a[:, j : j + 1] * (1.0 / row[:, j : j + 1])
        below = lax.broadcasted_iota(jnp.int32, (a.shape[0], 1), 0) > top
        a = a - jnp.where(below, factor, 0.0) * row
        if top == 7:
            done.append(a[0:8, :])
            a = a[8:, :]
    a = jnp.concatenate(done, axis=0)
    diagonal = jnp.sum(jnp.where(eye, a[:, 0:modes], 0.0), axis=1, keepdims=True)
    inverse = a[:, modes : 2 * modes] * (1.0 / jnp.sqrt(diagonal))
    mix = jnp.dot(inverse, k[0:modes, :], precision=HIGH, preferred_element_type=jnp.float32)[:, 0:total_rows]
    high = mix.astype(jnp.bfloat16)
    low = (mix - high.astype(jnp.float32)).astype(jnp.bfloat16)
    for fy in range(fy_count):
        block = rows_ref[:, fy * nx : (fy + 1) * nx]
        solved = jnp.dot(high, block, preferred_element_type=jnp.float32) + jnp.dot(
            low, block, preferred_element_type=jnp.float32
        )
        for c in range(nx // LANES):
            out[c, pl.ds(fy, modes, stride=fy_count), :] = solved[:, c * LANES : (c + 1) * LANES]
    for c in range(nx // LANES):
        basis_ref[:, c * LANES : (c + 1) * LANES] = out[c].astype(jnp.bfloat16)


def params(limit, collective_id=None):
    if collective_id is None:
        return pltpu.CompilerParams(vmem_limit_bytes=limit)
    return pltpu.CompilerParams(vmem_limit_bytes=limit, collective_id=collective_id, has_side_effects=True)


def local(n, snapshots, basis, mode_weights, land_mask, scale_index, scale_values):
    snaps, fields, cols, ny = snapshots.shape
    modes, _, own, nx = basis.shape
    win = own + 2 * HALO
    groups = LANES // win
    tiles = snaps * fields // groups
    fy_count = fields * own
    total_rows = modes + snaps
    total_cells = float(fields * nx * ny)
    limit = 48 * 1024 * 1024

    mask = jnp.broadcast_to(land_mask.astype(jnp.bfloat16)[None], (groups, cols, ny))
    pieces = jnp.concatenate([snapshots.reshape(tiles * groups, cols, ny), mask], axis=0)
    pieces = pieces.reshape(tiles + 1, groups, cols, ny)
    y = lax.broadcasted_iota(jnp.int32, (ny, n * LANES), 0)
    column = lax.broadcasted_iota(jnp.int32, (ny, n * LANES), 1)
    target, lane = column // LANES, column % LANES
    choices = []
    for g in range(groups):
        here = (lane >= g * win) & (lane < (g + 1) * win)
        choices.append((here & (y == target * own - HALO + lane - g * win)).astype(jnp.bfloat16))
    send = lax.dot_general(
        jnp.swapaxes(pieces, 1, 2).reshape((tiles + 1) * cols, groups * ny),
        jnp.concatenate(choices, axis=0),
        (((1,), (0,)), ((), ())),
        preferred_element_type=jnp.float32,
    ).astype(jnp.bfloat16).reshape(tiles + 1, cols, n * LANES)

    sems = [pltpu.SemaphoreType.DMA((n,)), pltpu.SemaphoreType.DMA((n,))]
    recv = pl.pallas_call(
        functools.partial(spread_kernel, n, cols),
        out_shape=jax.ShapeDtypeStruct((tiles + 1, nx, LANES), jnp.bfloat16),
        in_specs=[VMEM],
        out_specs=VMEM,
        scratch_shapes=[pltpu.VMEM((tiles + 1, nx, LANES), jnp.bfloat16)] + sems,
        compiler_params=params(limit, 0),
        name="spread",
    )(send)
    rows, part = pl.pallas_call(
        functools.partial(filter_kernel, win, groups),
        out_shape=(
            jax.ShapeDtypeStruct((total_rows, fy_count * nx), jnp.bfloat16),
            jax.ShapeDtypeStruct((total_rows, LANES), jnp.float32),
        ),
        in_specs=[VMEM] * 4,
        out_specs=(VMEM, VMEM),
        scratch_shapes=[
            pltpu.VMEM((nx // LANES, total_rows * fy_count, LANES), jnp.float32),
            pltpu.VMEM((5, nx, LANES), jnp.float32),
        ],
        compiler_params=params(limit),
        name="filter",
    )(recv, basis.reshape(modes * fy_count, nx), scale_index.reshape(1, ny), scale_values.reshape(1, -1))
    total = pl.pallas_call(
        functools.partial(sum_kernel, n),
        out_shape=jax.ShapeDtypeStruct((total_rows, LANES), jnp.float32),
        in_specs=[VMEM],
        out_specs=VMEM,
        scratch_shapes=[pltpu.VMEM((n, total_rows, LANES), jnp.float32)] + sems,
        compiler_params=params(limit, 1),
        name="total",
    )(part)
    new_basis, coefficients = pl.pallas_call(
        functools.partial(solve_kernel, total_cells, nx),
        out_shape=(
            jax.ShapeDtypeStruct((modes * fy_count, nx), jnp.bfloat16),
            jax.ShapeDtypeStruct((snaps, modes), jnp.float32),
        ),
        in_specs=[VMEM] * 3,
        out_specs=(VMEM, VMEM),
        scratch_shapes=[
            pltpu.VMEM((LANES, LANES), jnp.float32),
            pltpu.VMEM((LANES, LANES), jnp.float32),
            pltpu.VMEM((nx // LANES, modes * fy_count, LANES), jnp.float32),
        ],
        compiler_params=params(limit),
        name="solve",
    )(total, mode_weights.reshape(1, modes), rows)
    return new_basis.reshape(basis.shape), coefficients


def solution(mesh):
    placed = (
        P("group", None, "space", None),
        P("group", None, "space", None),
        P("group"),
        P("space", None),
        P(),
        P(),
    )
    return jax.shard_map(
        functools.partial(local, mesh.shape["space"]),
        mesh=mesh,
        in_specs=placed,
        out_specs=(P("group", None, "space", None), P("group", None)),
        check_vma=False,
    )
```

time: 176 us -> 55.8 us (0.32)
  the two profiles are of different devices: /device:TPU:0 before, /device:TPU:13 now
where the time goes in v1:
time: 55.8 us; the launch traced here: 55.6 us
  Pallas kernels  52 us (93%)
  other arithmetic  1.6 us (3%)
  matrix products  1.06 us (2%)
  between operations  0.83 us (1%)
    pallas_call x1, Pallas kernels, local(): pl.pallas_call(functools.partial(sum_kernel, n), out_shape=jax.ShapeDtype...  19 us
    pallas_call x1, Pallas kernels, local(): pl.pallas_call(functools.partial(spread_kernel, n, cols), out_shape=jax.S...  18.4 us
    pallas_call x1, Pallas kernels, local(): pl.pallas_call(functools.partial(solve_kernel, total_cells, nx), out_shap...  7.53 us
    pallas_call x1, Pallas kernels, local(): pl.pallas_call(functools.partial(filter_kernel, win, groups), out_shape=(...  7.07 us
    unnamed x5, other arithmetic  1.29 us

profile of v1, /device:TPU:13, one launch (start us, length us, event | category | flops | bytes accessed | tf_op | source)
XLA Modules:
  0.0 55.6 jit_solution(7464663248260758180)
XLA Ops:
  0.6 0.0 copy-start.5
  0.6 0.0 copy-start.4
  0.7 0.2 fusion.12
  0.9 0.3 fusion.11
  1.2 0.3 fusion.10
  1.5 0.3 fusion.9
  1.7 0.3 fusion.8
  2.0 0.3 fusion.7
  2.3 0.0 copy-done.5
  2.3 0.0 copy-done.4
  2.3 0.1 copy.8
  2.4 0.0 copy-start.2
  2.4 0.0 copy-start.3
  2.5 1.1 %convolution_convert_fusion = bf16[144,2048]{1,0:T(8,128)(2,1)S(1)} fusion(pred[768,2048]{1,0:T(8,128)(4,1)S(1)} %fusion.7, bf16[18,8,6,128]{3,2,1,0:T(8,128)(2,1)S(1)} %bitcast.22), kind=kOutput, calls=%fused_computation.13 | convolution fusion | flops 453279744 | bytes 2383872 | tf_op jit(solution)/shard_map/dot_general | solution.py:243
  3.5 0.0 copy-start
  3.5 0.0 copy-start.1
  3.5 18.4 %spread.1.recv_ref = bf16[9,256,128]{2,1,0:T(8,128)(2,1)S(1)} custom-call(bf16[9,16,2048]{2,1,0:T(8,128)(2,1)S(1)} %bitcast.17), custom_call_target="tpu_custom_call" | custom-call | tf_op jit(solution)/shard_map/spread/pallas_call | solution.py:251
  21.9 0.0 copy-done.2
  21.9 0.0 copy-done.3
  21.9 0.0 copy-done
  21.9 7.1 %filter.1 = (bf16[80,6144]{1,0:T(8,128)(2,1)S(1)}, f32[80,128]{1,0:T(8,128)S(1)}) custom-call(bf16[9,256,128]{2,1,0:T(8,128)(2,1)S(1)} %spread.1.recv_ref, bf16[1536,256]{1,0:T(8,128)(2,1)S(1)} %bitcast.16, s32[1,128]{1,0:T(1,128)S(1)} %bitcast.19, f32[1,16]{1,0:T(1,128)S(1)} %bitcast.20), custom_call_target="tpu_custom_call" | custom-call | tf_op jit(solution)/shard_map/filter/pallas_call | solution.py:260
  29.0 19.0 %total.1.gram_ref = f32[80,128]{1,0:T(8,128)S(1)} custom-call(f32[80,128]{1,0:T(8,128)S(1)} %get-tuple-element.6.part_ref), custom_call_target="tpu_custom_call" | custom-call | tf_op jit(solution)/shard_map/total/pallas_call | solution.py:275
  48.1 0.0 copy-done.1
  48.1 7.5 %solve.1 = (bf16[1536,256]{1,0:T(8,128)(2,1)}, f32[16,64]{1,0:T(8,128)}) custom-call(f32[80,128]{1,0:T(8,128)S(1)} %total.1.gram_ref, f32[1,64]{1,0:T(1,128)S(1)} %bitcast.18, bf16[80,6144]{1,0:T(8,128)(2,1)S(1)} %get-tuple-element.7.rows_ref), custom_call_target="tpu_custom_call" | custom-call | tf_op jit(solution)/shard_map/solve/pallas_call | solution.py:284
  (6 shorter events, 0.1 us)
Async XLA Ops:
  0.6 1.6 %copy-start.5 = (s32[16,128]{1,0:T(8,128)S(1)}, s32[16,128]{1,0:T(8,128)}, u32[]{:S(2)}) copy-start(s32[16,128]{1,0:T(8,128)} %param.9) | copy-start | bytes 24580
  0.6 1.7 %copy-start.4 = (bf16[16,3,16,128]{3,2,1,0:T(8,128)(2,1)S(1)}, bf16[16,3,16,128]{3,2,1,0:T(8,128)(2,1)}, u32[]{:S(2)}) copy-start(bf16[16,3,16,128]{3,2,1,0:T(8,128)(2,1)} %param.6) | copy-start | bytes 589828
  2.4 19.5 %copy-start.2 = (s32[128]{0:T(128)S(1)}, s32[128]{0:T(128)}, u32[]{:S(2)}) copy-start(s32[128]{0:T(128)} %param.10) | copy-start | bytes 1540
  2.4 19.5 %copy-start.3 = (f32[16]{0:T(128)S(1)}, f32[16]{0:T(128)}, u32[]{:S(2)}) copy-start(f32[16]{0:T(128)} %param.11) | copy-start | bytes 196
  3.5 18.4 %copy-start = (bf16[64,3,8,256]{3,2,1,0:T(8,128)(2,1)S(1)}, bf16[64,3,8,256]{3,2,1,0:T(8,128)(2,1)}, u32[]{:S(2)}) copy-start(bf16[64,3,8,256]{3,2,1,0:T(8,128)(2,1)} %param.7) | copy-start | bytes 2359300
  3.5 44.5 %copy-start.1 = (f32[64]{0:T(128)S(1)}, f32[64]{0:T(128)}, u32[]{:S(2)}) copy-start(f32[64]{0:T(128)} %param.8) | copy-start | bytes 772

commit v2 on v1

--- a/solution.py
+++ b/solution.py
@@ -74,29 +74,76 @@
     sent()
 
 
-def sum_kernel(n, part_ref, total_ref, land, send_sem, recv_sem):
+def sum_kernel(n, part_ref, total_ref, land, gather, send_part, recv_part, send_sum, recv_sum):
     me = lax.axis_index("space")
     group = lax.axis_index("group")
-    greet(n)
-
-    def make_copy(dst, slot):
+    bands = part_ref.shape[0] // 8
+    mine = lax.div(me * bands + n - 1, n)
+
+    def owner(band):
+        return lax.div(band * n, bands)
+
+    def band_rows(band):
+        return pl.ds(pl.multiple_of(band * 8, 8), 8)
+
+    def part_copy(band, slot):
         return pltpu.make_async_remote_copy(
-            src_ref=part_ref,
+            src_ref=part_ref.at[band_rows(band)],
             dst_ref=land.at[slot],
-            send_sem=send_sem.at[dst],
-            recv_sem=recv_sem.at[slot],
+            send_sem=send_part.at[band],
+            recv_sem=recv_part.at[slot],
+            device_id=(group, owner(band)),
+            device_id_type=MESH,
+        )
+
+    def sum_copy(band, dst):
+        return pltpu.make_async_remote_copy(
+            src_ref=gather.at[band_rows(band)],
+            dst_ref=gather.at[band_rows(band)],
+            send_sem=send_sum.at[dst],
+            recv_sem=recv_sum.at[band],
             device_id=(group, dst),
             device_id_type=MESH,
         )
 
-    arrived, sent = exchange(n, make_copy)
-    land[me] = part_ref[...]
-    arrived()
-    total = land[0]
-    for slot in range(1, n):
-        total = total + land[slot]
-    total_ref[...] = total
-    sent()
+    def others(act):
+        def body(band, carry):
+            @pl.when(owner(band) != me)
+            def _():
+                act(band)
+
+            return carry
+
+        lax.fori_loop(0, bands, body, 0)
+
+    def peers(act):
+        def body(step, carry):
+            act(peer(step, n))
+            return carry
+
+        lax.fori_loop(1, n, body, 0)
+
+    greet(n)
+    others(lambda band: part_copy(band, me).start())
+    owns = (mine < bands) & (owner(mine) == me)
+
+    @pl.when(owns)
+    def _():
+        land[me] = part_ref[band_rows(mine)]
+        peers(lambda source: part_copy(mine, source).wait_recv())
+        total = land[0]
+        for slot in range(1, n):
+            total = total + land[slot]
+        gather[band_rows(mine), :] = total
+        peers(lambda dst: sum_copy(mine, dst).start())
+
+    others(lambda band: sum_copy(band, me).wait_recv())
+    total_ref[...] = gather[...]
+    others(lambda band: part_copy(band, me).wait_send())
+
+    @pl.when(owns)
+    def _():
+        peers(lambda dst: sum_copy(mine, dst).wait_send())
 
 
 def filter_kernel(win, groups, recv_ref, basis_ref, index_ref, values_ref, rows_ref, gram_ref, stack, weight):
@@ -277,7 +324,14 @@
         out_shape=jax.ShapeDtypeStruct((total_rows, LANES), jnp.float32),
         in_specs=[VMEM],
         out_specs=VMEM,
-        scratch_shapes=[pltpu.VMEM((n, total_rows, LANES), jnp.float32)] + sems,
+        scratch_shapes=[
+            pltpu.VMEM((n, 8, LANES), jnp.float32),
+            pltpu.VMEM((total_rows, LANES), jnp.float32),
+            pltpu.SemaphoreType.DMA((total_rows // 8,)),
+            pltpu.SemaphoreType.DMA((n,)),
+            pltpu.SemaphoreType.DMA((n,)),
+            pltpu.SemaphoreType.DMA((total_rows // 8,)),
+        ],
         compiler_params=params(limit, 1),
         name="total",
     )(part)

time: 55.8 us -> 50.9 us (0.912)
  the two profiles are of different devices: /device:TPU:13 before, /device:TPU:0 now
where the time goes in v2:
time: 50.9 us; the launch traced here: 50.8 us
  Pallas kernels  47.2 us (93%)
  other arithmetic  1.6 us (3%)
  matrix products  1.06 us (2%)
  between operations  0.83 us (2%)
    pallas_call x1, Pallas kernels, local(): pl.pallas_call(functools.partial(spread_kernel, n, cols), out_shape=jax.S...  16.4 us
    pallas_call x1, Pallas kernels, local(): pl.pallas_call(functools.partial(sum_kernel, n), out_shape=jax.ShapeDtype...  16.2 us
    pallas_call x1, Pallas kernels, local(): pl.pallas_call(functools.partial(solve_kernel, total_cells, nx), out_shap...  7.53 us
    pallas_call x1, Pallas kernels, local(): pl.pallas_call(functools.partial(filter_kernel, win, groups), out_shape=(...  7.07 us
    unnamed x5, other arithmetic  1.29 us
    dot_general x1, matrix products, local(): lax.dot_general(jnp.swapaxes(pieces, 1, 2).reshape((tiles + 1) * cols, gr...  1.06 us

profile of v2, /device:TPU:0, one launch (start us, length us, event | category | flops | bytes accessed | tf_op | source)
XLA Modules:
  0.0 50.8 jit_solution(18235151979388982282)
XLA Ops:
  0.6 0.0 copy-start.5
  0.6 0.0 copy-start.4
  0.7 0.2 fusion.12
  0.9 0.3 fusion.11
  1.2 0.3 fusion.10
  1.5 0.3 fusion.9
  1.7 0.3 fusion.8
  2.0 0.3 fusion.7
  2.3 0.0 copy-done.5
  2.3 0.0 copy-done.4
  2.3 0.1 copy.8
  2.4 0.0 copy-start.2
  2.4 0.0 copy-start.3
  2.5 1.1 %convolution_convert_fusion = bf16[144,2048]{1,0:T(8,128)(2,1)S(1)} fusion(pred[768,2048]{1,0:T(8,128)(4,1)S(1)} %fusion.7, bf16[18,8,6,128]{3,2,1,0:T(8,128)(2,1)S(1)} %bitcast.22), kind=kOutput, calls=%fused_computation.13 | convolution fusion | flops 453279744 | bytes 2383872 | tf_op jit(solution)/shard_map/dot_general | solution.py:290
  3.5 0.0 copy-start
  3.5 0.0 copy-start.1
  3.5 16.4 %spread.1.recv_ref = bf16[9,256,128]{2,1,0:T(8,128)(2,1)S(1)} custom-call(bf16[9,16,2048]{2,1,0:T(8,128)(2,1)S(1)} %bitcast.17), custom_call_target="tpu_custom_call" | custom-call | tf_op jit(solution)/shard_map/spread/pallas_call | solution.py:298
  20.0 0.0 copy-done.2
  20.0 0.0 copy-done.3
  20.0 0.0 copy-done
  20.0 7.1 %filter.1 = (bf16[80,6144]{1,0:T(8,128)(2,1)S(1)}, f32[80,128]{1,0:T(8,128)S(1)}) custom-call(bf16[9,256,128]{2,1,0:T(8,128)(2,1)S(1)} %spread.1.recv_ref, bf16[1536,256]{1,0:T(8,128)(2,1)S(1)} %bitcast.16, s32[1,128]{1,0:T(1,128)S(1)} %bitcast.19, f32[1,16]{1,0:T(1,128)S(1)} %bitcast.20), custom_call_target="tpu_custom_call" | custom-call | tf_op jit(solution)/shard_map/filter/pallas_call | solution.py:307
  27.1 16.2 %total.1.gram_ref = f32[80,128]{1,0:T(8,128)S(1)} custom-call(f32[80,128]{1,0:T(8,128)S(1)} %get-tuple-element.6.part_ref), custom_call_target="tpu_custom_call" | custom-call | tf_op jit(solution)/shard_map/total/pallas_call | solution.py:322
  43.2 0.0 copy-done.1
  43.3 7.5 %solve.1 = (bf16[1536,256]{1,0:T(8,128)(2,1)}, f32[16,64]{1,0:T(8,128)}) custom-call(f32[80,128]{1,0:T(8,128)S(1)} %total.1.gram_ref, f32[1,64]{1,0:T(1,128)S(1)} %bitcast.18, bf16[80,6144]{1,0:T(8,128)(2,1)S(1)} %get-tuple-element.7.rows_ref), custom_call_target="tpu_custom_call" | custom-call | tf_op jit(solution)/shard_map/solve/pallas_call | solution.py:338
  (6 shorter events, 0.1 us)
Async XLA Ops:
  0.6 1.6 %copy-start.5 = (s32[16,128]{1,0:T(8,128)S(1)}, s32[16,128]{1,0:T(8,128)}, u32[]{:S(2)}) copy-start(s32[16,128]{1,0:T(8,128)} %param.9) | copy-start | bytes 24580
  0.6 1.7 %copy-start.4 = (bf16[16,3,16,128]{3,2,1,0:T(8,128)(2,1)S(1)}, bf16[16,3,16,128]{3,2,1,0:T(8,128)(2,1)}, u32[]{:S(2)}) copy-start(bf16[16,3,16,128]{3,2,1,0:T(8,128)(2,1)} %param.6) | copy-start | bytes 589828
  2.4 17.5 %copy-start.2 = (s32[128]{0:T(128)S(1)}, s32[128]{0:T(128)}, u32[]{:S(2)}) copy-start(s32[128]{0:T(128)} %param.10) | copy-start | bytes 1540
  2.4 17.5 %copy-start.3 = (f32[16]{0:T(128)S(1)}, f32[16]{0:T(128)}, u32[]{:S(2)}) copy-start(f32[16]{0:T(128)} %param.11) | copy-start | bytes 196
  3.5 16.5 %copy-start = (bf16[64,3,8,256]{3,2,1,0:T(8,128)(2,1)S(1)}, bf16[64,3,8,256]{3,2,1,0:T(8,128)(2,1)}, u32[]{:S(2)}) copy-start(bf16[64,3,8,256]{3,2,1,0:T(8,128)(2,1)} %param.7) | copy-start | bytes 2359300
  3.5 39.7 %copy-start.1 = (f32[64]{0:T(128)S(1)}, f32[64]{0:T(128)}, u32[]{:S(2)}) copy-start(f32[64]{0:T(128)} %param.8) | copy-start | bytes 772

commit v3 on v2

v3 whole, which is shorter than its diff:
```python
import functools
import math

import jax
import jax.numpy as jnp
from jax import lax
from jax.experimental import pallas as pl
from jax.experimental.pallas import tpu as pltpu
from jax.sharding import PartitionSpec as P

PASS_COEFS = (1.0, 0.95, 0.85, 0.7, 0.5, 0.3)
HALO = len(PASS_COEFS)
LANES = 128
HIGH = lax.Precision.HIGHEST
MESH = pl.DeviceIdType.MESH
VMEM = pl.BlockSpec(memory_space=pltpu.VMEM)


def peer(step, n):
    return lax.rem(lax.axis_index("space") + step, n)


def greet(n):
    group = lax.axis_index("group")
    barrier = pltpu.get_barrier_semaphore()

    def signal(step, carry):
        pl.semaphore_signal(barrier, inc=1, device_id=(group, peer(step, n)), device_id_type=MESH)
        return carry

    lax.fori_loop(1, n, signal, 0)
    pl.semaphore_wait(barrier, n - 1)


def band_sum(n, part_ref, total_ref, land, gather, send_part, recv_part, send_sum, recv_sum):
    me = lax.axis_index("space")
    group = lax.axis_index("group")
    bands = part_ref.shape[0] // 8
    mine = lax.div(me * bands + n - 1, n)

    def owner(band):
        return lax.div(band * n, bands)

    def band_rows(band):
        return pl.ds(pl.multiple_of(band * 8, 8), 8)

    def part_copy(band, slot):
        return pltpu.make_async_remote_copy(
            src_ref=part_ref.at[band_rows(band)],
            dst_ref=land.at[slot],
            send_sem=send_part.at[band],
            recv_sem=recv_part.at[slot],
            device_id=(group, owner(band)),
            device_id_type=MESH,
        )

    def sum_copy(band, dst):
        return pltpu.make_async_remote_copy(
            src_ref=gather.at[band_rows(band)],
            dst_ref=gather.at[band_rows(band)],
            send_sem=send_sum.at[dst],
            recv_sem=recv_sum.at[band],
            device_id=(group, dst),
            device_id_type=MESH,
        )

    def others(act):
        def body(band, carry):
            @pl.when(owner(band) != me)
            def _():
                act(band)

            return carry

        lax.fori_loop(0, bands, body, 0)

    def peers(act):
        def body(step, carry):
            act(peer(step, n))
            return carry

        lax.fori_loop(1, n, body, 0)

    others(lambda band: part_copy(band, me).start())
    owns = (mine < bands) & (owner(mine) == me)

    @pl.when(owns)
    def _():
        land[me] = part_ref[band_rows(mine)]
        peers(lambda source: part_copy(mine, source).wait_recv())
        total = land[0]
        for slot in range(1, n):
            total = total + land[slot]
        gather[band_rows(mine), :] = total
        peers(lambda dst: sum_copy(mine, dst).start())

    others(lambda band: sum_copy(band, me).wait_recv())
    total_ref[...] = gather[...]
    others(lambda band: part_copy(band, me).wait_send())

    @pl.when(owns)
    def _():
        peers(lambda dst: sum_copy(mine, dst).wait_send())


def swap_groups(parts, width):
    parts = list(parts)
    size = parts[0].shape[1]
    lane = lax.broadcasted_iota(jnp.int32, parts[0].shape, 1)
    bit = 1
    while bit < len(parts):
        shift = bit * width
        upper = lax.rem(lax.div(lane, shift), 2) == 1
        for s in range(len(parts)):
            if not s & bit:
                a, b = parts[s], parts[s | bit]
                parts[s] = jnp.where(upper, pltpu.roll(b, shift, 1), a)
                parts[s | bit] = jnp.where(upper, b, pltpu.roll(a, size - shift, 1))
        bit *= 2
    return parts


def project_kernel(
    n,
    cols,
    snaps_ref,
    mask_ref,
    basis_ref,
    index_ref,
    values_ref,
    rows_ref,
    total_ref,
    wide,
    spread,
    weight,
    packed,
    land,
    stack,
    part,
    band_land,
    gather,
    edge_send,
    edge_recv,
    data_send,
    data_recv,
    send_part,
    recv_part,
    send_sum,
    recv_sum,
):
    me = lax.axis_index("space")
    group = lax.axis_index("group")
    count = snaps_ref.shape[0] // cols
    ny, nx = snaps_ref.shape[1], basis_ref.shape[1]
    own = ny // n
    groups = LANES // own
    modes_rows = basis_ref.shape[0]
    total_rows, fy_count = rows_ref.shape[0], rows_ref.shape[1] // nx
    modes = modes_rows // fy_count
    y_tiles, x_tiles = ny // LANES, nx // LANES

    for c in range(y_tiles):
        spread[c] = snaps_ref[:, c * LANES : (c + 1) * LANES].astype(jnp.float32)
    for x in range(cols):
        for c in range(y_tiles):
            wide[HALO + x, 0:count, c * LANES : (c + 1) * LANES] = spread[
                c, pl.ds(x, count, stride=cols), :
            ].astype(jnp.bfloat16)
        line = mask_ref[x : x + 1, :].astype(jnp.float32)
        wide[HALO + x, count : count + 16, :] = jnp.broadcast_to(line, (16, ny)).astype(jnp.bfloat16)

    greet(n)

    def edge_copy(first, to, where, who):
        return pltpu.make_async_remote_copy(
            src_ref=wide.at[pl.ds(first, HALO)],
            dst_ref=wide.at[pl.ds(to, HALO)],
            send_sem=edge_send.at[where],
            recv_sem=edge_recv.at[where],
            device_id=(group, who),
            device_id_type=MESH,
        )

    to_left = edge_copy(HALO, HALO + cols, 0, peer(n - 1, n))
    to_right = edge_copy(cols, 0, 1, peer(1, n))
    to_left.start()
    to_right.start()

    for c in range(x_tiles):
        stack[c, 0:modes_rows, :] = basis_ref[:, c * LANES : (c + 1) * LANES].astype(jnp.float32)
    for fy in range(fy_count):
        for c in range(x_tiles):
            at = fy * nx + c * LANES
            rows_ref[0:modes, at : at + LANES] = stack[c, pl.ds(fy, modes, stride=fy_count), :].astype(jnp.bfloat16)
    part[...] = jnp.zeros_like(part)
    part[0:modes, 0:modes] = lax.dot_general(
        rows_ref[0:modes, :], rows_ref[0:modes, :], (((1,), (1,)), ((), ())), preferred_element_type=jnp.float32
    )
    lat = jnp.zeros((1, ny), jnp.float32)
    for level in range(values_ref.shape[1]):
        lat = lat + jnp.where(index_ref[...] == level, values_ref[0:1, level : level + 1], 0.0)
    lane = lax.broadcasted_iota(jnp.int32, (8, ny), 1)

    to_left.wait()
    to_right.wait()

    def north(a):
        return pltpu.roll(a, ny - 1, 1)

    def south(a):
        return pltpu.roll(a, 1, 1)

    last = cols + 2 * HALO
    ocean = [wide[x, count : count + 16, :].astype(jnp.float32)[0:8] for x in range(last)]
    for x in range(1, last - 1):
        base = ocean[x] * lat
        weight[0, x] = base * ocean[x + 1]
        weight[1, x] = base * ocean[x - 1]
        weight[2, x] = jnp.where(lane == ny - 1, 0.0, base * north(ocean[x]))
        weight[3, x] = jnp.where(lane == 0, 0.0, base * south(ocean[x]))
        weight[4, x] = ocean[x]

    @pl.loop(0, count // 16)
    def _(block):
        start = pl.multiple_of(block * 16, 16)
        both = [wide[x, pl.ds(start, 16), :].astype(jnp.float32) for x in range(last)]
        for side in range(2):
            f = [b[side * 8 : side * 8 + 8] for b in both]
            for i, coef in enumerate(PASS_COEFS):
                new = list(f)
                for x in range(i + 1, last - i - 1):
                    centre = f[x]
                    flux = weight[0, x] * (f[x + 1] - centre) + weight[1, x] * (f[x - 1] - centre)
                    flux = flux + weight[2, x] * (north(centre) - centre) + weight[3, x] * (south(centre) - centre)
                    new[x] = centre + coef * flux
                f = new
            for x in range(cols):
                done = weight[4, HALO + x] * f[HALO + x]
                at = pl.multiple_of(x * count + start + side * 8, 8)
                for c in range(y_tiles):
                    spread[c, pl.ds(at, 8), :] = done[:, c * LANES : (c + 1) * LANES]

    for t in range(count // groups):
        for c in range(y_tiles):
            parts = [spread[c, pl.ds(t * groups + g, cols, stride=count), :] for g in range(groups)]
            for g, piece in enumerate(swap_groups(parts, own)):
                packed[c * groups + g, t] = piece.astype(jnp.bfloat16)

    def data_copy(dst, slot):
        return pltpu.make_async_remote_copy(
            src_ref=packed.at[dst],
            dst_ref=land.at[:, pl.ds(pl.multiple_of(slot * cols, cols), cols), :],
            send_sem=data_send.at[dst],
            recv_sem=data_recv.at[slot],
            device_id=(group, dst),
            device_id_type=MESH,
        )

    def each_peer(act):
        def body(step, carry):
            act(peer(step, n))
            return carry

        lax.fori_loop(1, n, body, 0)

    each_peer(lambda dst: data_copy(dst, me).start())
    land[:, pl.ds(pl.multiple_of(me * cols, cols), cols), :] = packed[me]
    each_peer(lambda source: data_copy(source, source).wait_recv())

    for t in range(count // groups):
        turned = land[t].astype(jnp.float32).T
        for c in range(x_tiles):
            stack[c, modes_rows + t * LANES : modes_rows + (t + 1) * LANES, :] = turned[:, c * LANES : (c + 1) * LANES]
    for fy in range(fy_count):
        for c in range(x_tiles):
            at = fy * nx + c * LANES
            rows_ref[modes:total_rows, at : at + LANES] = stack[
                c, pl.ds(modes_rows + fy, total_rows - modes, stride=fy_count), :
            ].astype(jnp.bfloat16)
    part[modes:total_rows, 0:total_rows] = lax.dot_general(
        rows_ref[modes:total_rows, :], rows_ref[...], (((1,), (1,)), ((), ())), preferred_element_type=jnp.float32
    )
    band_sum(n, part, total_ref, band_land, gather, send_part, recv_part, send_sum, recv_sum)
    each_peer(lambda dst: data_copy(dst, me).wait_send())


def solve_kernel(total_cells, nx, gram_ref, weights_ref, rows_ref, basis_ref, coef_ref, k_t, full, out):
    modes = weights_ref.shape[1]
    total_rows = gram_ref.shape[0]
    fy_count = rows_ref.shape[1] // nx
    eye = (
        lax.broadcasted_iota(jnp.int32, (modes, modes), 0) == lax.broadcasted_iota(jnp.int32, (modes, modes), 1)
    )
    full[...] = jnp.zeros_like(full)
    full[0:total_rows, :] = gram_ref[...]
    row = lax.broadcasted_iota(jnp.int32, full.shape, 0)
    column = lax.broadcasted_iota(jnp.int32, full.shape, 1)
    full[...] = jnp.where((row < modes) & (column >= modes), full[...].T, full[...])
    coefficients = full[modes:total_rows, 0:modes] * (1.0 / math.sqrt(total_cells))
    coef_ref[...] = coefficients
    k_t[...] = jnp.zeros_like(k_t)
    k_t[0:modes, 0:modes] = jnp.where(eye, weights_ref[...], 0.0)
    k_t[modes:total_rows, 0:modes] = coefficients.astype(jnp.bfloat16).astype(jnp.float32)
    k = k_t[...].T
    half = jnp.dot(full[...], k_t[...], precision=HIGH, preferred_element_type=jnp.float32)
    gram = jnp.dot(k, half, precision=HIGH, preferred_element_type=jnp.float32)[0:modes, 0:modes] * (1.0 / total_cells)

    a = jnp.concatenate([gram, jnp.where(eye, 1.0, 0.0)], axis=1)
    done = []
    for j in range(modes):
        top = j % 8
        row = a[top : top + 1, :]
        factor = a[:, j : j + 1] * (1.0 / row[:, j : j + 1])
        below = lax.broadcasted_iota(jnp.int32, (a.shape[0], 1), 0) > top
        a = a - jnp.where(below, factor, 0.0) * row
        if top == 7:
            done.append(a[0:8, :])
            a = a[8:, :]
    a = jnp.concatenate(done, axis=0)
    diagonal = jnp.sum(jnp.where(eye, a[:, 0:modes], 0.0), axis=1, keepdims=True)
    inverse = a[:, modes : 2 * modes] * (1.0 / jnp.sqrt(diagonal))
    mix = jnp.dot(inverse, k[0:modes, :], precision=HIGH, preferred_element_type=jnp.float32)[:, 0:total_rows]
    high = mix.astype(jnp.bfloat16)
    low = (mix - high.astype(jnp.float32)).astype(jnp.bfloat16)
    for fy in range(fy_count):
        block = rows_ref[:, fy * nx : (fy + 1) * nx]
        solved = jnp.dot(high, block, preferred_element_type=jnp.float32) + jnp.dot(
            low, block, preferred_element_type=jnp.float32
        )
        for c in range(nx // LANES):
            out[c, pl.ds(fy, modes, stride=fy_count), :] = solved[:, c * LANES : (c + 1) * LANES]
    for c in range(nx // LANES):
        basis_ref[:, c * LANES : (c + 1) * LANES] = out[c].astype(jnp.bfloat16)


def params(limit, collective_id=None):
    if collective_id is None:
        return pltpu.CompilerParams(vmem_limit_bytes=limit)
    return pltpu.CompilerParams(vmem_limit_bytes=limit, collective_id=collective_id, has_side_effects=True)


def local(n, snapshots, basis, mode_weights, land_mask, scale_index, scale_values):
    snaps, fields, cols, ny = snapshots.shape
    modes, _, own, nx = basis.shape
    count = snaps * fields
    fy_count = fields * own
    total_rows = modes + snaps
    total_cells = float(fields * nx * ny)
    limit = 48 * 1024 * 1024
    groups = LANES // own
    bands = total_rows // 8

    rows, total = pl.pallas_call(
        functools.partial(project_kernel, n, cols),
        out_shape=(
            jax.ShapeDtypeStruct((total_rows, fy_count * nx), jnp.bfloat16),
            jax.ShapeDtypeStruct((total_rows, LANES), jnp.float32),
        ),
        in_specs=[VMEM] * 5,
        out_specs=(VMEM, VMEM),
        scratch_shapes=[
            pltpu.VMEM((cols + 2 * HALO, count + 16, ny), jnp.bfloat16),
            pltpu.VMEM((ny // LANES, count * cols, LANES), jnp.float32),
            pltpu.VMEM((5, cols + 2 * HALO, 8, ny), jnp.float32),
            pltpu.VMEM((n, count // groups, cols, LANES), jnp.bfloat16),
            pltpu.VMEM((count // groups, nx, LANES), jnp.bfloat16),
            pltpu.VMEM((nx // LANES, total_rows * fy_count, LANES), jnp.float32),
            pltpu.VMEM((total_rows, LANES), jnp.float32),
            pltpu.VMEM((n, 8, LANES), jnp.float32),
            pltpu.VMEM((total_rows, LANES), jnp.float32),
        ]
        + [pltpu.SemaphoreType.DMA((k,)) for k in (2, 2, n, n, bands, n, n, bands)],
        compiler_params=params(limit, 0),
        name="project",
    )(
        snapshots.reshape(count * cols, ny),
        land_mask,
        basis.reshape(modes * fy_count, nx),
        scale_index.reshape(1, ny),
        scale_values.reshape(1, -1),
    )
    new_basis, coefficients = pl.pallas_call(
        functools.partial(solve_kernel, total_cells, nx),
        out_shape=(
            jax.ShapeDtypeStruct((modes * fy_count, nx), jnp.bfloat16),
            jax.ShapeDtypeStruct((snaps, modes), jnp.float32),
        ),
        in_specs=[VMEM] * 3,
        out_specs=(VMEM, VMEM),
        scratch_shapes=[
            pltpu.VMEM((LANES, LANES), jnp.float32),
            pltpu.VMEM((LANES, LANES), jnp.float32),
            pltpu.VMEM((nx // LANES, modes * fy_count, LANES), jnp.float32),
        ],
        compiler_params=params(limit),
        name="solve",
    )(total, mode_weights.reshape(1, modes), rows)
    return new_basis.reshape(basis.shape), coefficients


def solution(mesh):
    placed = (
        P("group", None, "space", None),
        P("group", None, "space", None),
        P("group"),
        P("space", None),
        P(),
        P(),
    )
    return jax.shard_map(
        functools.partial(local, mesh.shape["space"]),
        mesh=mesh,
        in_specs=placed,
        out_specs=(P("group", None, "space", None), P("group", None)),
        check_vma=False,
    )
```

time: 50.9 us -> 40 us (0.79)
  Pallas kernels: 47.2 us -> 35.7 us
  local copies, waits for them, and re-layouts: 0.12 us -> 3.39 us
  other arithmetic: 1.6 us -> 0 us
  matrix products: 1.06 us -> 0 us
    pallas_call x3 -> x1, Pallas kernels: 39.6 us -> 28.2 us  [local(): pl.pallas_call(functools.partial(project_kernel, n, cols), out_shape=(jax...]
    unnamed x12, local copies, waits for them, and re-layouts: 0.03 us -> 3.39 us
    unnamed x5 -> x0, other arithmetic: 1.29 us -> none
    dot_general x1 -> x0, matrix products: 1.06 us -> none  [local(): lax.dot_general(jnp.swapaxes(pieces, 1, 2).reshape((tiles + 1) * cols, gr...]
where the time goes in v3:
time: 40 us; the launch traced here: 39.8 us
  Pallas kernels  35.7 us (89%)
  local copies, waits for them, and re-layouts  3.39 us (8%)
  between operations  0.67 us (2%)
    pallas_call x1, Pallas kernels, local(): pl.pallas_call(functools.partial(project_kernel, n, cols), out_shape=(jax...  28.2 us
    pallas_call x1, Pallas kernels, local(): pl.pallas_call(functools.partial(solve_kernel, total_cells, nx), out_shap...  7.58 us
    unnamed x12, local copies, waits for them, and re-layouts  3.39 us

profile of v3, /device:TPU:0, one launch (start us, length us, event | category | flops | bytes accessed | tf_op | source)
XLA Modules:
  0.0 39.8 jit_solution(9096489672263746087)
XLA Ops:
  0.6 0.0 copy-start.2
  0.6 0.0 copy-start.4
  0.7 0.0 copy-start.5
  0.7 0.7 %copy-done.2 = s32[16,128]{1,0:T(8,128)S(1)} copy-done((s32[16,128]{1,0:T(8,128)S(1)}, s32[16,128]{1,0:T(8,128)}, u32[]{:S(2)}) %copy-start.2) | copy-done | bytes 8216
  1.3 0.0 copy-done.4
  1.3 0.0 copy-done.5
  1.3 0.0 copy-start
  1.3 1.1 %copy-done = bf16[64,3,8,256]{3,2,1,0:T(8,128)(2,1)S(1)} copy-done((bf16[64,3,8,256]{3,2,1,0:T(8,128)(2,1)S(1)}, bf16[64,3,8,256]{3,2,1,0:T(8,128)(2,1)}, u32[]{:S(2)}) %copy-start) | copy-done | bytes 786456
  2.5 0.0 copy-start.1
  2.5 0.9 %copy-done.1 = bf16[16,3,16,128]{3,2,1,0:T(8,128)(2,1)S(1)} copy-done((bf16[16,3,16,128]{3,2,1,0:T(8,128)(2,1)S(1)}, bf16[16,3,16,128]{3,2,1,0:T(8,128)(2,1)}, u32[]{:S(2)}) %copy-start.1) | copy-done | bytes 196632
  3.4 28.2 %project.1 = (bf16[80,6144]{1,0:T(8,128)(2,1)S(1)}, f32[80,128]{1,0:T(8,128)S(1)}) custom-call(bf16[768,128]{1,0:T(8,128)(2,1)S(1)} %bitcast.7, s32[16,128]{1,0:T(8,128)S(1)} %copy-done.2, bf16[1536,256]{1,0:T(8,128)(2,1)S(1)} %bitcast.6, s32[1,128]{1,0:T(1,128)S(1)} %bitcast.9, f32[1,16]{1,0:T(1,128)S(1)} %bitcast.10), custom_call_target="tpu_custom_call" | custom-call | tf_op jit(solution)/shard_map/project/pallas_call | solution.py:353
  31.6 0.0 copy-start.3
  31.6 0.6 %copy-done.3 = f32[64]{0:T(128)S(1)} copy-done((f32[64]{0:T(128)S(1)}, f32[64]{0:T(128)}, u32[]{:S(2)}) %copy-start.3) | copy-done | bytes 280
  32.2 7.6 %solve.1 = (bf16[1536,256]{1,0:T(8,128)(2,1)}, f32[16,64]{1,0:T(8,128)}) custom-call(f32[80,128]{1,0:T(8,128)S(1)} %get-tuple-element.6.gram_ref, f32[1,64]{1,0:T(1,128)S(1)} %bitcast.8, bf16[80,6144]{1,0:T(8,128)(2,1)S(1)} %get-tuple-element.7.rows_ref), custom_call_target="tpu_custom_call" | custom-call | tf_op jit(solution)/shard_map/solve/pallas_call | solution.py:382
Async XLA Ops:
  0.6 0.7 %copy-start.2 = (s32[16,128]{1,0:T(8,128)S(1)}, s32[16,128]{1,0:T(8,128)}, u32[]{:S(2)}) copy-start(s32[16,128]{1,0:T(8,128)} %mask_ref.1) | copy-start | bytes 24580
  0.6 0.7 %copy-start.4 = (s32[128]{0:T(128)S(1)}, s32[128]{0:T(128)}, u32[]{:S(2)}) copy-start(s32[128]{0:T(128)} %param.10) | copy-start | bytes 1540
  0.7 0.7 %copy-start.5 = (f32[16]{0:T(128)S(1)}, f32[16]{0:T(128)}, u32[]{:S(2)}) copy-start(f32[16]{0:T(128)} %param.11) | copy-start | bytes 196
  1.3 1.1 %copy-start = (bf16[64,3,8,256]{3,2,1,0:T(8,128)(2,1)S(1)}, bf16[64,3,8,256]{3,2,1,0:T(8,128)(2,1)}, u32[]{:S(2)}) copy-start(bf16[64,3,8,256]{3,2,1,0:T(8,128)(2,1)} %param.7) | copy-start | bytes 2359300
  2.5 0.9 %copy-start.1 = (bf16[16,3,16,128]{3,2,1,0:T(8,128)(2,1)S(1)}, bf16[16,3,16,128]{3,2,1,0:T(8,128)(2,1)}, u32[]{:S(2)}) copy-start(bf16[16,3,16,128]{3,2,1,0:T(8,128)(2,1)} %param.6) | copy-start | bytes 589828
  31.6 0.7 %copy-start.3 = (f32[64]{0:T(128)S(1)}, f32[64]{0:T(128)}, u32[]{:S(2)}) copy-start(f32[64]{0:T(128)} %param.8) | copy-start | bytes 772

commit v4 on v3

--- a/solution.py
+++ b/solution.py
@@ -14,6 +14,7 @@
 HIGH = lax.Precision.HIGHEST
 MESH = pl.DeviceIdType.MESH
 VMEM = pl.BlockSpec(memory_space=pltpu.VMEM)
+HBM = pl.BlockSpec(memory_space=pltpu.HBM)
 
 
 def peer(step, n):
@@ -29,13 +30,12 @@
         return carry
 
     lax.fori_loop(1, n, signal, 0)
-    pl.semaphore_wait(barrier, n - 1)
-
-
-def band_sum(n, part_ref, total_ref, land, gather, send_part, recv_part, send_sum, recv_sum):
+    return barrier
+
+
+def band_sum(n, bands, part_ref, land, gather, send_part, recv_part, send_sum, recv_sum):
     me = lax.axis_index("space")
     group = lax.axis_index("group")
-    bands = part_ref.shape[0] // 8
     mine = lax.div(me * bands + n - 1, n)
 
     def owner(band):
@@ -81,26 +81,31 @@
 
         lax.fori_loop(1, n, body, 0)
 
-    others(lambda band: part_copy(band, me).start())
     owns = (mine < bands) & (owner(mine) == me)
 
-    @pl.when(owns)
-    def _():
-        land[me] = part_ref[band_rows(mine)]
-        peers(lambda source: part_copy(mine, source).wait_recv())
-        total = land[0]
-        for slot in range(1, n):
-            total = total + land[slot]
-        gather[band_rows(mine), :] = total
-        peers(lambda dst: sum_copy(mine, dst).start())
-
-    others(lambda band: sum_copy(band, me).wait_recv())
-    total_ref[...] = gather[...]
-    others(lambda band: part_copy(band, me).wait_send())
-
-    @pl.when(owns)
-    def _():
-        peers(lambda dst: sum_copy(mine, dst).wait_send())
+    def start():
+        others(lambda band: part_copy(band, me).start())
+
+    def reduce():
+        @pl.when(owns)
+        def _():
+            land[me] = part_ref[band_rows(mine)]
+            peers(lambda source: part_copy(mine, source).wait_recv())
+            total = land[0]
+            for slot in range(1, n):
+                total = total + land[slot]
+            gather[band_rows(mine), :] = total
+            peers(lambda dst: sum_copy(mine, dst).start())
+
+    def finish():
+        others(lambda band: sum_copy(band, me).wait_recv())
+        others(lambda band: part_copy(band, me).wait_send())
+
+        @pl.when(owns)
+        def _():
+            peers(lambda dst: sum_copy(mine, dst).wait_send())
+
+    return start, reduce, finish
 
 
 def swap_groups(parts, width):
@@ -123,13 +128,16 @@
 def project_kernel(
     n,
     cols,
-    snaps_ref,
-    mask_ref,
-    basis_ref,
+    snaps_hbm,
+    mask_hbm,
+    basis_hbm,
     index_ref,
     values_ref,
     rows_ref,
     total_ref,
+    snaps_ref,
+    mask_ref,
+    basis_ref,
     wide,
     spread,
     weight,
@@ -139,6 +147,9 @@
     part,
     band_land,
     gather,
+    late,
+    late_land,
+    loaded,
     edge_send,
     edge_recv,
     data_send,
@@ -147,9 +158,18 @@
     recv_part,
     send_sum,
     recv_sum,
+    late_send,
+    late_recv,
 ):
     me = lax.axis_index("space")
     group = lax.axis_index("group")
+    loads = [
+        pltpu.make_async_copy(src, dst, loaded.at[i])
+        for i, (src, dst) in enumerate(((snaps_hbm, snaps_ref), (mask_hbm, mask_ref), (basis_hbm, basis_ref)))
+    ]
+    for load in loads:
+        load.start()
+    barrier = greet(n)
     count = snaps_ref.shape[0] // cols
     ny, nx = snaps_ref.shape[1], basis_ref.shape[1]
     own = ny // n
@@ -159,6 +179,8 @@
     modes = modes_rows // fy_count
     y_tiles, x_tiles = ny // LANES, nx // LANES
 
+    loads[0].wait()
+    loads[1].wait()
     for c in range(y_tiles):
         spread[c] = snaps_ref[:, c * LANES : (c + 1) * LANES].astype(jnp.float32)
     for x in range(cols):
@@ -169,7 +191,7 @@
         line = mask_ref[x : x + 1, :].astype(jnp.float32)
         wide[HALO + x, count : count + 16, :] = jnp.broadcast_to(line, (16, ny)).astype(jnp.bfloat16)
 
-    greet(n)
+    pl.semaphore_wait(barrier, n - 1)
 
     def edge_copy(first, to, where, who):
         return pltpu.make_async_remote_copy(
@@ -186,6 +208,7 @@
     to_left.start()
     to_right.start()
 
+    loads[2].wait()
     for c in range(x_tiles):
         stack[c, 0:modes_rows, :] = basis_ref[:, c * LANES : (c + 1) * LANES].astype(jnp.float32)
     for fy in range(fy_count):
@@ -196,6 +219,10 @@
     part[0:modes, 0:modes] = lax.dot_general(
         rows_ref[0:modes, :], rows_ref[0:modes, :], (((1,), (1,)), ((), ())), preferred_element_type=jnp.float32
     )
+    start_bands, reduce_bands, finish_bands = band_sum(
+        n, modes // 8, part, band_land, gather, send_part, recv_part, send_sum, recv_sum
+    )
+    start_bands()
     lat = jnp.zeros((1, ny), jnp.float32)
     for level in range(values_ref.shape[1]):
         lat = lat + jnp.where(index_ref[...] == level, values_ref[0:1, level : level + 1], 0.0)
@@ -265,6 +292,7 @@
 
     each_peer(lambda dst: data_copy(dst, me).start())
     land[:, pl.ds(pl.multiple_of(me * cols, cols), cols), :] = packed[me]
+    reduce_bands()
     each_peer(lambda source: data_copy(source, source).wait_recv())
 
     for t in range(count // groups):
@@ -277,10 +305,31 @@
             rows_ref[modes:total_rows, at : at + LANES] = stack[
                 c, pl.ds(modes_rows + fy, total_rows - modes, stride=fy_count), :
             ].astype(jnp.bfloat16)
-    part[modes:total_rows, 0:total_rows] = lax.dot_general(
+    late[...] = jnp.zeros_like(late)
+    late[:, 0:total_rows] = lax.dot_general(
         rows_ref[modes:total_rows, :], rows_ref[...], (((1,), (1,)), ((), ())), preferred_element_type=jnp.float32
     )
-    band_sum(n, part, total_ref, band_land, gather, send_part, recv_part, send_sum, recv_sum)
+
+    def late_copy(dst, slot):
+        return pltpu.make_async_remote_copy(
+            src_ref=late,
+            dst_ref=late_land.at[slot],
+            send_sem=late_send.at[dst],
+            recv_sem=late_recv.at[slot],
+            device_id=(group, dst),
+            device_id_type=MESH,
+        )
+
+    each_peer(lambda dst: late_copy(dst, me).start())
+    late_land[me] = late[...]
+    finish_bands()
+    total_ref[0:modes, :] = gather[...]
+    each_peer(lambda source: late_copy(source, source).wait_recv())
+    total = late_land[0]
+    for slot in range(1, n):
+        total = total + late_land[slot]
+    total_ref[modes:total_rows, :] = total
+    each_peer(lambda dst: late_copy(dst, me).wait_send())
     each_peer(lambda dst: data_copy(dst, me).wait_send())
 
 
@@ -346,9 +395,9 @@
     fy_count = fields * own
     total_rows = modes + snaps
     total_cells = float(fields * nx * ny)
-    limit = 48 * 1024 * 1024
+    limit = 60 * 1024 * 1024
     groups = LANES // own
-    bands = total_rows // 8
+    bands = modes // 8
 
     rows, total = pl.pallas_call(
         functools.partial(project_kernel, n, cols),
@@ -356,20 +405,25 @@
             jax.ShapeDtypeStruct((total_rows, fy_count * nx), jnp.bfloat16),
             jax.ShapeDtypeStruct((total_rows, LANES), jnp.float32),
         ),
-        in_specs=[VMEM] * 5,
+        in_specs=[HBM] * 3 + [VMEM] * 2,
         out_specs=(VMEM, VMEM),
         scratch_shapes=[
+            pltpu.VMEM((count * cols, ny), jnp.bfloat16),
+            pltpu.VMEM((cols, ny), jnp.int32),
+            pltpu.VMEM((modes * fy_count, nx), jnp.bfloat16),
             pltpu.VMEM((cols + 2 * HALO, count + 16, ny), jnp.bfloat16),
             pltpu.VMEM((ny // LANES, count * cols, LANES), jnp.float32),
             pltpu.VMEM((5, cols + 2 * HALO, 8, ny), jnp.float32),
             pltpu.VMEM((n, count // groups, cols, LANES), jnp.bfloat16),
             pltpu.VMEM((count // groups, nx, LANES), jnp.bfloat16),
             pltpu.VMEM((nx // LANES, total_rows * fy_count, LANES), jnp.float32),
-            pltpu.VMEM((total_rows, LANES), jnp.float32),
+            pltpu.VMEM((modes, LANES), jnp.float32),
             pltpu.VMEM((n, 8, LANES), jnp.float32),
-            pltpu.VMEM((total_rows, LANES), jnp.float32),
+            pltpu.VMEM((modes, LANES), jnp.float32),
+            pltpu.VMEM((snaps, LANES), jnp.float32),
+            pltpu.VMEM((n, snaps, LANES), jnp.float32),
         ]
-        + [pltpu.SemaphoreType.DMA((k,)) for k in (2, 2, n, n, bands, n, n, bands)],
+        + [pltpu.SemaphoreType.DMA((k,)) for k in (3, 2, 2, n, n, bands, n, n, bands, n, n)],
         compiler_params=params(limit, 0),
         name="project",
     )(

time: 40 us -> 37.5 us (0.938)
  local copies, waits for them, and re-layouts: 3.39 us -> 0 us
  Pallas kernels: 35.7 us -> 36.7 us
    unnamed x12 -> x0, local copies, waits for them, and re-layouts: 3.39 us -> none
    pallas_call x1, Pallas kernels: 7.58 us -> 8.83 us  [local(): pl.pallas_call(functools.partial(solve_kernel, total_cells, nx), out_shap...]
where the time goes in v4:
time: 37.5 us; the launch traced here: 37.3 us
  Pallas kernels  36.7 us (98%)
  between operations  0.64 us (2%)
    pallas_call x1, Pallas kernels, local(): pl.pallas_call(functools.partial(project_kernel, n, cols), out_shape=(jax...  27.9 us
    pallas_call x1, Pallas kernels, local(): pl.pallas_call(functools.partial(solve_kernel, total_cells, nx), out_shap...  8.83 us

profile of v4, /device:TPU:0, one launch (start us, length us, event | category | flops | bytes accessed | tf_op | source)
XLA Modules:
  0.0 37.3 jit_solution(15393823323569710404)
XLA Ops:
  0.6 27.9 %project.1 = (bf16[80,6144]{1,0:T(8,128)(2,1)}, f32[80,128]{1,0:T(8,128)}) custom-call(bf16[768,128]{1,0:T(8,128)(2,1)} %bitcast.7, s32[16,128]{1,0:T(8,128)} %mask_hbm.1, bf16[1536,256]{1,0:T(8,128)(2,1)} %bitcast.6, s32[1,128]{1,0:T(1,128)} %bitcast.9, f32[1,16]{1,0:T(1,128)} %bitcast.10), custom_call_target="tpu_custom_call" | custom-call | tf_op jit(solution)/shard_map/project/pallas_call | solution.py:402
  28.5 8.8 %solve.1 = (bf16[1536,256]{1,0:T(8,128)(2,1)}, f32[16,64]{1,0:T(8,128)}) custom-call(f32[80,128]{1,0:T(8,128)} %get-tuple-element.6.gram_ref, f32[1,64]{1,0:T(1,128)} %bitcast.8, bf16[80,6144]{1,0:T(8,128)(2,1)} %get-tuple-element.7.rows_ref), custom_call_target="tpu_custom_call" | custom-call | tf_op jit(solution)/shard_map/solve/pallas_call | solution.py:436

commit v5 on v4

--- a/solution.py
+++ b/solution.py
@@ -356,13 +356,20 @@
 
     a = jnp.concatenate([gram, jnp.where(eye, 1.0, 0.0)], axis=1)
     done = []
-    for j in range(modes):
+    for j in range(0, modes, 2):
         top = j % 8
-        row = a[top : top + 1, :]
-        factor = a[:, j : j + 1] * (1.0 / row[:, j : j + 1])
-        below = lax.broadcasted_iota(jnp.int32, (a.shape[0], 1), 0) > top
-        a = a - jnp.where(below, factor, 0.0) * row
-        if top == 7:
+        first, second = a[top : top + 1, :], a[top + 1 : top + 2, :]
+        column, beside = a[:, j : j + 1], a[:, j + 1 : j + 2]
+        inv_first = 1.0 / first[:, j : j + 1]
+        across = first[:, j + 1 : j + 2]
+        scale = second[:, j : j + 1] * inv_first
+        inv_second = 1.0 / (second[:, j + 1 : j + 2] - scale * across)
+        factor = column * inv_first
+        factor_next = (beside - factor * across) * inv_second
+        second = second - scale * first
+        row_at = lax.broadcasted_iota(jnp.int32, (a.shape[0], 1), 0)
+        a = a - jnp.where(row_at > top, factor, 0.0) * first - jnp.where(row_at > top + 1, factor_next, 0.0) * second
+        if top == 6:
             done.append(a[0:8, :])
             a = a[8:, :]
     a = jnp.concatenate(done, axis=0)

time: 37.5 us -> 39.1 us (1.043)
  Pallas kernels: 36.7 us -> 38.3 us
    pallas_call x1, Pallas kernels: 8.83 us -> 10.4 us  [local(): pl.pallas_call(functools.partial(solve_kernel, total_cells, nx), out_shap...]
where the time goes in v5:
time: 39.1 us; the launch traced here: 39 us
  Pallas kernels  38.3 us (98%)
  between operations  0.64 us (2%)
    pallas_call x1, Pallas kernels, local(): pl.pallas_call(functools.partial(project_kernel, n, cols), out_shape=(jax...  27.9 us
    pallas_call x1, Pallas kernels, local(): pl.pallas_call(functools.partial(solve_kernel, total_cells, nx), out_shap...  10.4 us

profile of v5, /device:TPU:0, one launch (start us, length us, event | category | flops | bytes accessed | tf_op | source)
XLA Modules:
  0.0 39.0 jit_solution(10176929971120860909)
XLA Ops:
  0.6 27.9 %project.1 = (bf16[80,6144]{1,0:T(8,128)(2,1)}, f32[80,128]{1,0:T(8,128)}) custom-call(bf16[768,128]{1,0:T(8,128)(2,1)} %bitcast.7, s32[16,128]{1,0:T(8,128)} %mask_hbm.1, bf16[1536,256]{1,0:T(8,128)(2,1)} %bitcast.6, s32[1,128]{1,0:T(1,128)} %bitcast.9, f32[1,16]{1,0:T(1,128)} %bitcast.10), custom_call_target="tpu_custom_call" | custom-call | tf_op jit(solution)/shard_map/project/pallas_call | solution.py:409
  28.5 10.4 %solve.1 = (bf16[1536,256]{1,0:T(8,128)(2,1)}, f32[16,64]{1,0:T(8,128)}) custom-call(f32[80,128]{1,0:T(8,128)} %get-tuple-element.6.gram_ref, f32[1,64]{1,0:T(1,128)} %bitcast.8, bf16[80,6144]{1,0:T(8,128)(2,1)} %get-tuple-element.7.rows_ref), custom_call_target="tpu_custom_call" | custom-call | tf_op jit(solution)/shard_map/solve/pallas_call | solution.py:443

commit v6 on v4

--- a/solution.py
+++ b/solution.py
@@ -359,9 +359,9 @@
     for j in range(modes):
         top = j % 8
         row = a[top : top + 1, :]
-        factor = a[:, j : j + 1] * (1.0 / row[:, j : j + 1])
+        scaled = row * (1.0 / row[:, j : j + 1])
         below = lax.broadcasted_iota(jnp.int32, (a.shape[0], 1), 0) > top
-        a = a - jnp.where(below, factor, 0.0) * row
+        a = a - jnp.where(below, a[:, j : j + 1], 0.0) * scaled
         if top == 7:
             done.append(a[0:8, :])
             a = a[8:, :]

time: 37.5 us -> 37.6 us (level)
  no operation moved by 1% of the time
where the time goes in v6:
time: 37.6 us; the launch traced here: 37.4 us
  Pallas kernels  36.8 us (98%)
  between operations  0.64 us (2%)
    pallas_call x1, Pallas kernels, local(): pl.pallas_call(functools.partial(project_kernel, n, cols), out_shape=(jax...  27.9 us
    pallas_call x1, Pallas kernels, local(): pl.pallas_call(functools.partial(solve_kernel, total_cells, nx), out_shap...  8.89 us

profile of v6, /device:TPU:0, one launch (start us, length us, event | category | flops | bytes accessed | tf_op | source)
XLA Modules:
  0.0 37.4 jit_solution(10161043105437577101)
XLA Ops:
  0.6 27.9 %project.1 = (bf16[80,6144]{1,0:T(8,128)(2,1)}, f32[80,128]{1,0:T(8,128)}) custom-call(bf16[768,128]{1,0:T(8,128)(2,1)} %bitcast.7, s32[16,128]{1,0:T(8,128)} %mask_hbm.1, bf16[1536,256]{1,0:T(8,128)(2,1)} %bitcast.6, s32[1,128]{1,0:T(1,128)} %bitcast.9, f32[1,16]{1,0:T(1,128)} %bitcast.10), custom_call_target="tpu_custom_call" | custom-call | tf_op jit(solution)/shard_map/project/pallas_call | solution.py:402
  28.5 8.9 %solve.1 = (bf16[1536,256]{1,0:T(8,128)(2,1)}, f32[16,64]{1,0:T(8,128)}) custom-call(f32[80,128]{1,0:T(8,128)} %get-tuple-element.6.gram_ref, f32[1,64]{1,0:T(1,128)} %bitcast.8, bf16[80,6144]{1,0:T(8,128)(2,1)} %get-tuple-element.7.rows_ref), custom_call_target="tpu_custom_call" | custom-call | tf_op jit(solution)/shard_map/solve/pallas_call | solution.py:436
